TPU v7x, 32 devices: a whole 2x2x4 slice. The times are simulated.
32 devices in a mesh: dom: 32 (over z, y, x, core).
Axes of the slice: x: 2, y: 2, z: 4, core: 2. Of those that a mesh axis runs over, the one named last changes fastest.
Arguments:
- q_state: float32 [9, 56, 4096], P(None, None, 'dom'), may hold values from -6 to 6
- star_mats: float32 [3, 9, 9, 4096], P(None, None, None, 'dom'), may hold values from -3 to 3
- flux_minus: float32 [4, 9, 9, 4096], P(None, None, None, 'dom'), may hold values from -2 to 2
- flux_plus: float32 [4, 9, 9, 4096], P(None, None, None, 'dom'), may hold values from -2 to 2
- time_limit: float32 [4096], P('dom'), may hold values from 0.25 to 3.6
- deriv_mats: float32 [3, 56, 56], replicated, may hold values from -0.75 to 0.75
- volume_mats: float32 [3, 56, 56], replicated, may hold values from -0.75 to 0.75
- face_proj: float32 [4, 21, 56], replicated, may hold values from -0.75 to 0.75
- face_lift: float32 [4, 56, 21], replicated, may hold values from -1.25 to 1.25
- face_link: int32 [4, 4096], P(None, 'dom'), may hold values from -1 to 895, as said below
- face_orient: int32 [4, 4096], P(None, 'dom'), may hold values from 0 to 2
- send_face: int32 [6, 2048], P(None, 'dom'), may hold values from -1 to 511, as said below
Outputs:
- q_new: float32 [9, 56, 4096], P(None, None, 'dom')
Inputs may be any that keep to these rules, and one draw needn't show every extreme that they name: For face f of element e of a partition, v = face_link[f, d * 128 + e]: -1 is an absorbing boundary; v < 512 names face v // 128 of element v % 128 of the same partition; otherwise v = 512 + k * 64 + s names slot s of received block k, and s is below the number of faces that the partition at offset o_k sends it. No block holds more than 64 faces, and some blocks are full. `send_face`: row k of a partition's 64 columns lists the faces f * 128 + e that it sends to the partition at offset - o_k, then -1 in the unused slots; their number equals what that partition reads from the block; no face stands twice on a partition.
All inputs are finite; a program needn't handle non-finite values.
Results may differ from a plain program's by a relative error of at most 0.0003.
Values sent between devices are 32-bit elements; how exact they have to be, the bound alone decides.
A program may use at most 128 MiB of HBM per device.

v0:
```python
import functools
import math

import jax
import jax.numpy as jnp
import numpy as np
from jax import lax
from jax.experimental import pallas as pl
from jax.experimental.pallas import tpu as pltpu
from jax.sharding import PartitionSpec as P

ORDER = 6
REACH = 3
FINE_DEV = 64
NODE_PAD = 24
F32 = jnp.float32
BF16 = jnp.bfloat16
MESH = pl.DeviceIdType.MESH


def rotation_table(node_count):
    degree = 0
    while (degree + 1) * (degree + 2) // 2 < node_count:
        degree += 1
    node_pairs = [
        (across, upward) for across in range(degree + 1) for upward in range(degree + 1 - across)
    ]
    lookup = {pair: number for number, pair in enumerate(node_pairs)}
    tables = []
    for rotations in range(3):
        new_order = []
        for node_pair in node_pairs:
            moved_pair = (node_pair[1], node_pair[0])
            for repeat in range(rotations):
                moved_pair = (moved_pair[1], degree - moved_pair[0] - moved_pair[1])
            new_order.append(lookup[moved_pair])
        tables.append(new_order)
    return np.array(tables, dtype=np.int32)


def round_up(value, step):
    return (value + step - 1) // step * step


def radices(count):
    out = []
    while count > 1:
        radix = max([r for r in range(2, 9) if count % r == 0], default=count)
        out.append(radix)
        count //= radix
    return out


def offset_of(position):
    return position - REACH if position < REACH else position - REACH + 1


def split(value):
    high = value.astype(BF16)
    low = (value - high.astype(F32)).astype(BF16)
    return high, low


def dot(a, b):
    return jnp.dot(a, b, preferred_element_type=F32)


def kernel(
    count,
    nq,
    nb,
    nf,
    q_ref,
    star_ref,
    minus_ref,
    plus_ref,
    limit_ref,
    deriv_ref,
    volume_ref,
    proj_ref,
    lift_ref,
    link_ref,
    orient_ref,
    send_ref,
    compact_ref,
    rotate_ref,
    out_ref,
    a_der,
    a_vol,
    a_proj,
    a_lift,
    s_local,
    s_remote,
    t_send,
    series,
    b_mat,
    r_mat,
    vol,
    own,
    ic_two,
    io,
    faces,
    pool,
    picked,
    turned,
    across,
    b_lift,
    base,
    min_out,
    min_in,
    send_buf,
    recv_buf,
    min_send_sem,
    min_recv_sem,
    send_sem,
    recv_sem,
):
    elems = q_ref.shape[2]
    lanes = lax.broadcasted_iota(jnp.int32, (1, elems), 1)
    is_fine = lanes < FINE_DEV
    me = lax.axis_index("dom")
    bp = b_mat.shape[0] // 3
    rows_c = pool.shape[0] // 2
    half = rows_c // 2
    digits = radices(count)

    def peer_of(number, step):
        stride = math.prod(digits[:number])
        radix = digits[number]
        digit = lax.rem(me // stride, radix)
        return me + (lax.rem(digit + step, radix) - digit) * stride

    barrier = pltpu.get_barrier_semaphore()
    expected = 0
    for number, radix in enumerate(digits):
        for step in range(1, radix):
            pl.semaphore_signal(
                barrier, inc=1, device_id=(peer_of(number, step),), device_id_type=MESH
            )
            expected += 1
    for position in range(2 * REACH):
        target = me - offset_of(position)

        @pl.when((target >= 0) & (target < count))
        def _():
            pl.semaphore_signal(barrier, inc=1, device_id=(target,), device_id_type=MESH)

    least = jnp.where(is_fine, limit_ref[...], limit_ref[...] * 0.5)
    least = jnp.broadcast_to(jnp.min(least, axis=1, keepdims=True), (8, elems))

    below = jnp.minimum(me, REACH)
    above = jnp.minimum(count - 1 - me, REACH)
    pl.semaphore_wait(barrier, expected + below + above)

    def min_copy(number, step):
        return pltpu.make_async_remote_copy(
            src_ref=min_out.at[number],
            dst_ref=min_in.at[number, step - 1],
            send_sem=min_send_sem.at[number, step - 1],
            recv_sem=min_recv_sem.at[number, step - 1],
            device_id=(peer_of(number, step),),
            device_id_type=MESH,
        )

    def min_start(number, value):
        min_out[number] = value
        for step in range(1, digits[number]):
            min_copy(number, step).start()

    def min_finish(number, value):
        for step in range(1, digits[number]):
            min_copy(number, step).wait_recv()
        for step in range(1, digits[number]):
            value = jnp.minimum(value, min_in[number, step - 1])
        return value

    if digits:
        min_start(0, least)

    def wide(x, width):
        high = x.astype(BF16).astype(F32)
        low = x - high
        if width > x.shape[1]:
            z = jnp.zeros((x.shape[0], width - x.shape[1]), F32)
            parts = [high, z, high, z, low, z]
        else:
            parts = [high, high, low]
        return jnp.concatenate(parts, axis=1)

    for d in range(3):
        r_mat[d * nb : (d + 1) * nb, 0 : 3 * bp] = wide(deriv_ref[d], bp)
    a_der[...] = r_mat[0 : 3 * nb, 0 : 3 * bp].astype(BF16)
    for d in range(3):
        r_mat[d * nb : (d + 1) * nb, 0 : 3 * bp] = wide(volume_ref[d], bp)
    a_vol[...] = r_mat[0 : 3 * nb, 0 : 3 * bp].astype(BF16)
    r_mat[0 : 4 * NODE_PAD, 0 : 3 * bp] = jnp.zeros((4 * NODE_PAD, 3 * bp), F32)
    for f in range(4):
        r_mat[f * NODE_PAD : f * NODE_PAD + nf, 0 : 3 * bp] = wide(proj_ref[:, f, :], bp)
    a_proj[...] = r_mat[0 : 4 * NODE_PAD, 0 : 3 * bp].astype(BF16)
    r_mat[0 : 4 * NODE_PAD, 0 : 128] = jnp.zeros((4 * NODE_PAD, 128), F32)
    for f in range(4):
        r_mat[f * NODE_PAD : f * NODE_PAD + nf, 0:nb] = lift_ref[:, f, :]
    turned_lift = jnp.transpose(r_mat[0 : 4 * NODE_PAD, 0:128])[0:nb]
    a_lift[...] = wide(turned_lift, 4 * NODE_PAD).astype(BF16)

    def fill(target_q, x):
        high, low = split(jnp.concatenate([x, jnp.zeros((bp - nb, elems), F32)], axis=0))
        b_mat[0:bp, target_q * elems : (target_q + 1) * elems] = high
        b_mat[bp : 2 * bp, target_q * elems : (target_q + 1) * elems] = low
        b_mat[2 * bp : 3 * bp, target_q * elems : (target_q + 1) * elems] = high

    def starred(a_ref, store):
        r_mat[...] = dot(a_ref[...], b_mat[...])

        def group(g, carry):
            sums = [None] * 3
            for d in range(3):
                for q in range(nq):
                    block = r_mat[d * nb : (d + 1) * nb, q * elems : (q + 1) * elems]
                    for i in range(3):
                        row = star_ref[g * 3 + i, q, d : d + 1, :]
                        term = row * block
                        sums[i] = term if sums[i] is None else sums[i] + term
            for i in range(3):
                store(g * 3 + i, sums[i])
            return carry

        lax.fori_loop(0, nq // 3, group, 0)

    def taylor():
        def step(k, carry):
            for q in range(nq):
                fill(q, series[k, q])

            def keep(p, value):
                series[k + 1, p] = -value

            starred(a_der, keep)
            return carry

        lax.fori_loop(0, ORDER - 1, step, 0)

    for q in range(nq):
        series[0, q] = q_ref[q]

    if digits:
        least = min_finish(0, least)
        if len(digits) > 1:
            min_start(1, least)

    taylor()

    numbers = lax.broadcasted_iota(jnp.int32, (128, elems), 0)
    own_faces = s_local.shape[0]
    for f in range(4):
        link = link_ref[f : f + 1, :]
        for v in range(0, own_faces, 128):
            s_local[v : v + 128, f * elems : (f + 1) * elems] = jnp.where(
                numbers + v == link, 1.0, 0.0
            ).astype(BF16)
        for v in range(0, s_remote.shape[0], 128):
            s_remote[v : v + 128, f * elems : (f + 1) * elems] = jnp.where(
                numbers + (v + own_faces) == link, 1.0, 0.0
            ).astype(BF16)
    for g in range(REACH):
        sends = jnp.concatenate([send_ref[2 * g : 2 * g + 1, :], send_ref[2 * g + 1 : 2 * g + 2, :]], axis=1)
        for v in range(0, own_faces, 128):
            t_send[v : v + 128, g * elems : (g + 1) * elems] = jnp.where(
                numbers + v == sends, 1.0, 0.0
            ).astype(BF16)
    faces[...] = jnp.zeros(faces.shape, F32)
    for stage in range(2):
        for position in range(2 * REACH):
            source = me + offset_of(position)

            @pl.when((source < 0) | (source >= count))
            def _():
                recv_buf[stage, position] = jnp.zeros(recv_buf.shape[2:], F32)

    for number in range(1, len(digits)):
        least = min_finish(number, least)
        if number + 1 < len(digits):
            min_start(number + 1, least)
    step_fine = least[0:1, :]

    weights = []
    weights_two = []
    power = step_fine
    for k in range(ORDER):
        weights.append(power * (1.0 / math.factorial(k + 1)))
        weights_two.append(weights[-1] * float(2 ** (k + 1) - 1))
        power = power * step_fine

    def block_copy(stage, position):
        return pltpu.make_async_remote_copy(
            src_ref=send_buf.at[stage, position],
            dst_ref=recv_buf.at[stage, position],
            send_sem=send_sem.at[stage, position],
            recv_sem=recv_sem.at[stage, position],
            device_id=(me - offset_of(position),),
            device_id_type=MESH,
        )

    def flux(solver_ref, data_ref, first):
        def face(f, carry):
            sums = [None] * nq
            for q in range(nq):
                block = data_ref[f, q * NODE_PAD : (q + 1) * NODE_PAD, :]
                for p in range(nq):
                    term = solver_ref[p, q, pl.ds(f, 1), :] * block
                    sums[p] = term if sums[p] is None else sums[p] + term
            spot = pl.ds(pl.multiple_of(f * NODE_PAD, 8), NODE_PAD)
            for p in range(nq):
                if first:
                    across[p, spot, :] = sums[p]
                else:
                    across[p, spot, :] = across[p, spot, :] + sums[p]
            return carry

        lax.fori_loop(0, 4, face, 0)

    def stage_work(stage):
        projected = dot(a_proj[...], b_mat[...])
        for f in range(4):
            for q in range(nq):
                faces[f, q * NODE_PAD : (q + 1) * NODE_PAD, :] = projected[
                    f * NODE_PAD : (f + 1) * NODE_PAD, q * elems : (q + 1) * elems
                ]
        for f in range(4):
            high, low = split(faces[f])
            pool[0:rows_c, f * elems : (f + 1) * elems] = dot(compact_ref[...], high).astype(BF16)
            pool[rows_c : 2 * rows_c, f * elems : (f + 1) * elems] = dot(
                compact_ref[...], low
            ).astype(BF16)
        for g in range(REACH):
            packed = dot(pool[...], t_send[:, g * elems : (g + 1) * elems])
            packed = packed[0:rows_c] + packed[rows_c : 2 * rows_c]
            upper, lower = packed[0:half], packed[half:rows_c]
            send_buf[stage, 2 * g] = jnp.where(is_fine, upper, pltpu.roll(lower, FINE_DEV, 1))
            send_buf[stage, 2 * g + 1] = jnp.where(is_fine, pltpu.roll(upper, FINE_DEV, 1), lower)
            for position in (2 * g, 2 * g + 1):
                target = me - offset_of(position)

                @pl.when((target >= 0) & (target < count))
                def _():
                    block_copy(stage, position).start()

        picked[...] = dot(pool[...], s_local[...])
        if stage == 0:
            own[...] = faces[...]
        else:
            for f in range(4):
                own[f] = jnp.where(is_fine, faces[f], faces[f] + own[f])
            for q in range(nq):
                fill(q, io[q])

        def keep(p, value):
            vol[p] = value

        starred(a_vol, keep)
        flux(minus_ref, own, True)

        for position in range(2 * REACH):
            source = me + offset_of(position)

            @pl.when((source >= 0) & (source < count))
            def _():
                block_copy(stage, position).wait_recv()

        for g in range(REACH):
            first, second = recv_buf[stage, 2 * g], recv_buf[stage, 2 * g + 1]
            upper = jnp.where(is_fine, first, pltpu.roll(second, FINE_DEV, 1))
            lower = jnp.where(is_fine, pltpu.roll(first, FINE_DEV, 1), second)
            high, low = split(jnp.concatenate([upper, lower], axis=0))
            pool[0:rows_c, g * elems : (g + 1) * elems] = high
            pool[rows_c : 2 * rows_c, g * elems : (g + 1) * elems] = low
        remote = s_remote.shape[0]
        total = (picked[...] + dot(pool[:, 0:remote], s_remote[...])).astype(BF16)
        rows_n = rotate_ref.shape[0] // 3
        for f in range(4):
            three = dot(rotate_ref[...], total[:, f * elems : (f + 1) * elems])
            code = orient_ref[f : f + 1, :]
            new = jnp.where(
                code == 0,
                three[0:rows_n],
                jnp.where(code == 1, three[rows_n : 2 * rows_n], three[2 * rows_n :]),
            )
            if stage == 0:
                turned[f] = new
            else:
                turned[f] = jnp.where(is_fine, new, new + turned[f])
        flux(plus_ref, turned, False)
        for p in range(nq):
            high, low = split(across[p])
            rows = 4 * NODE_PAD
            b_lift[0:rows, p * elems : (p + 1) * elems] = high
            b_lift[rows : 2 * rows, p * elems : (p + 1) * elems] = low
            b_lift[2 * rows : 3 * rows, p * elems : (p + 1) * elems] = high
        return dot(a_lift[...], b_lift[...])

    def weighted(q, table):
        total = table[0] * series[0, q]
        for k in range(1, ORDER):
            total = total + table[k] * series[k, q]
        return total

    for q in range(nq):
        one = weighted(q, weights)
        two = weighted(q, weights_two)
        fill(q, one)
        ic_two[q] = jnp.where(is_fine, 0.0, two)
        io[q] = jnp.where(is_fine, 0.0, one + two)
    lifted = stage_work(0)
    for p in range(nq):
        mid = q_ref[p] + vol[p] - lifted[:, p * elems : (p + 1) * elems]
        base[p] = jnp.where(is_fine, mid, q_ref[p])
        series[0, p] = jnp.where(is_fine, mid, 0.0)
    taylor()
    for q in range(nq):
        one = weighted(q, weights)
        fill(q, one + ic_two[q])
        io[q] = one + io[q]
    lifted = stage_work(1)
    for p in range(nq):
        out_ref[p] = base[p] + vol[p] - lifted[:, p * elems : (p + 1) * elems]

    for number, radix in enumerate(digits):
        for step in range(1, radix):
            min_copy(number, step).wait_send()
    for stage in range(2):
        for position in range(2 * REACH):
            target = me - offset_of(position)

            @pl.when((target >= 0) & (target < count))
            def _():
                block_copy(stage, position).wait_send()


def local(count, *args):
    q_state, face_proj, send_face = args[0], args[7], args[11]
    nq, nb, elems = q_state.shape
    nf = face_proj.shape[1]
    slots = send_face.shape[0] * send_face.shape[1]
    bp = round_up(nb, 16)
    rows_n = round_up(nq * NODE_PAD, 16)
    rows_c = round_up(nq * nf, 32)
    compact = np.zeros((rows_c, rows_n), np.float32)
    rotate = np.zeros((3 * rows_n, 2 * rows_c), np.float32)
    table = rotation_table(nf)
    for q in range(nq):
        for n in range(nf):
            compact[q * nf + n, q * NODE_PAD + n] = 1
            for h in range(3):
                rotate[h * rows_n + q * NODE_PAD + n, q * nf + table[h, n]] = 1
                rotate[h * rows_n + q * NODE_PAD + n, rows_c + q * nf + table[h, n]] = 1
    args = list(args)
    for number in (1, 2, 3):
        args[number] = jnp.transpose(args[number], (1, 2, 0, 3))
    args[4] = args[4].reshape(1, elems)
    args[7] = jnp.transpose(args[7], (1, 0, 2))
    args[8] = jnp.transpose(args[8], (2, 0, 1))
    args += [jnp.asarray(compact, BF16), jnp.asarray(rotate, BF16)]
    rounds = max(len(radices(count)), 1)
    widest = max([r - 1 for r in radices(count)] + [1])
    vm = pltpu.VMEM
    scratch = [
        vm((3 * nb, 3 * bp), BF16),
        vm((3 * nb, 3 * bp), BF16),
        vm((4 * NODE_PAD, 3 * bp), BF16),
        vm((nb, 12 * NODE_PAD), BF16),
        vm((4 * elems, 4 * elems), BF16),
        vm((slots, 4 * elems), BF16),
        vm((4 * elems, slots), BF16),
        vm((ORDER, nq, nb, elems), F32),
        vm((3 * bp, nq * elems), BF16),
        vm((3 * nb, nq * elems), F32),
        vm((nq, nb, elems), F32),
        vm((4, rows_n, elems), F32),
        vm((nq, nb, elems), F32),
        vm((nq, nb, elems), F32),
        vm((4, rows_n, elems), F32),
        vm((2 * rows_c, 4 * elems), BF16),
        vm((2 * rows_c, 4 * elems), F32),
        vm((4, rows_n, elems), F32),
        vm((nq, 4 * NODE_PAD, elems), F32),
        vm((12 * NODE_PAD, nq * elems), BF16),
        vm((nq, nb, elems), F32),
        vm((rounds, 8, elems), F32),
        vm((rounds, widest, 8, elems), F32),
        vm((2, 2 * REACH, rows_c // 2, elems), F32),
        vm((2, 2 * REACH, rows_c // 2, elems), F32),
        pltpu.SemaphoreType.DMA((rounds, widest)),
        pltpu.SemaphoreType.DMA((rounds, widest)),
        pltpu.SemaphoreType.DMA((2, 2 * REACH)),
        pltpu.SemaphoreType.DMA((2, 2 * REACH)),
    ]
    return pl.pallas_call(
        functools.partial(kernel, count, nq, nb, nf),
        out_shape=jax.ShapeDtypeStruct(q_state.shape, F32),
        in_specs=[pl.BlockSpec(memory_space=pltpu.VMEM)] * len(args),
        out_specs=pl.BlockSpec(memory_space=pltpu.VMEM),
        scratch_shapes=scratch,
        compiler_params=pltpu.CompilerParams(
            collective_id=0, has_side_effects=True, vmem_limit_bytes=40 * 1024 * 1024
        ),
    )(*args)


def solution(mesh):
    placed = (
        P(None, None, "dom"),
        P(None, None, None, "dom"),
        P(None, None, None, "dom"),
        P(None, None, None, "dom"),
        P("dom"),
        P(),
        P(),
        P(),
        P(),
        P(None, "dom"),
        P(None, "dom"),
        P(None, "dom"),
    )
    count = mesh.shape["dom"]
    return jax.shard_map(
        functools.partial(local, count),
        mesh=mesh,
        in_specs=placed,
        out_specs=P(None, None, "dom"),
        check_vma=False,
    )
```

profile of v0, /device:TPU:0, one launch (start us, length us, event | category | flops | bytes accessed | tf_op | source)
XLA Modules:
  0.0 46.5 jit_solution(14997229211157176399)
XLA Ops:
  0.0 0.0 copy-start.12
  0.0 0.0 copy-start.10
  0.0 0.0 copy-start.11
  0.0 0.0 copy-start.13
  0.0 0.7 %copy-done.12 = s32[4,128]{1,0:T(4,128)S(1)} copy-done((s32[4,128]{1,0:T(4,128)S(1)}, s32[4,128]{1,0:T(4,128)}, u32[]{:S(2)}) %copy-start.12) | copy-done | bytes 2072
  0.7 0.0 copy-done.10
  0.7 0.0 copy-done.11
  0.7 0.0 copy-done.13
  0.7 0.0 copy-start
  0.7 1.0 %copy-done = bf16[672,384]{1,0:T(8,128)(2,1)S(1)} copy-done((bf16[672,384]{1,0:T(8,128)(2,1)S(1)}, bf16[672,384]{1,0:T(8,128)(2,1)}, u32[]{:S(2)}) %copy-start) | copy-done | bytes 516120
  1.8 0.0 copy-start.1
  1.8 0.9 %copy-done.1 = f32[9,56,128]{2,1,0:T(8,128)S(1)} copy-done((f32[9,56,128]{2,1,0:T(8,128)S(1)}, f32[9,56,128]{2,1,0:T(8,128)}, u32[]{:S(2)}) %copy-start.1) | copy-done | bytes 258072
  2.7 0.0 copy-start.2
  2.7 0.9 %copy-done.2 = f32[3,9,9,128]{3,0,2,1:T(4,128)S(1)} copy-done((f32[3,9,9,128]{3,0,2,1:T(4,128)S(1)}, f32[3,9,9,128]{3,0,2,1:T(4,128)}, u32[]{:S(2)}) %copy-start.2) | copy-done | bytes 124440
  3.6 0.0 copy-start.3
  3.6 0.9 %copy-done.3 = f32[4,9,9,128]{3,0,2,1:T(4,128)S(1)} copy-done((f32[4,9,9,128]{3,0,2,1:T(4,128)S(1)}, f32[4,9,9,128]{3,0,2,1:T(4,128)}, u32[]{:S(2)}) %copy-start.3) | copy-done | bytes 165912
  4.5 0.0 copy-start.4
  4.5 0.9 %copy-done.4 = f32[4,9,9,128]{3,0,2,1:T(4,128)S(1)} copy-done((f32[4,9,9,128]{3,0,2,1:T(4,128)S(1)}, f32[4,9,9,128]{3,0,2,1:T(4,128)}, u32[]{:S(2)}) %copy-start.4) | copy-done | bytes 165912
  5.5 0.0 copy-start.5
  5.5 0.9 %copy-done.5 = bf16[192,224]{1,0:T(8,128)(2,1)S(1)} copy-done((bf16[192,224]{1,0:T(8,128)(2,1)S(1)}, bf16[192,224]{1,0:T(8,128)(2,1)}, u32[]{:S(2)}) %copy-start.5) | copy-done | bytes 86040
  6.3 0.0 copy-start.6
  6.4 0.9 %copy-done.6 = f32[3,56,56]{2,1,0:T(8,128)S(1)} copy-done((f32[3,56,56]{2,1,0:T(8,128)S(1)}, f32[3,56,56]{2,1,0:T(8,128)}, u32[]{:S(2)}) %copy-start.6) | copy-done | bytes 37656
  7.2 0.0 copy-start.7
  7.2 0.9 %copy-done.7 = f32[3,56,56]{2,1,0:T(8,128)S(1)} copy-done((f32[3,56,56]{2,1,0:T(8,128)S(1)}, f32[3,56,56]{2,1,0:T(8,128)}, u32[]{:S(2)}) %copy-start.7) | copy-done | bytes 37656
  8.1 0.0 copy-start.8
  8.1 0.8 %copy-done.8 = f32[4,21,56]{2,0,1:T(4,128)S(1)} copy-done((f32[4,21,56]{2,0,1:T(4,128)S(1)}, f32[4,21,56]{2,0,1:T(4,128)}, u32[]{:S(2)}) %copy-start.8) | copy-done | bytes 18840
  8.9 0.0 copy-start.9
  8.9 0.8 %copy-done.9 = f32[4,56,21]{1,0,2:T(4,128)S(1)} copy-done((f32[4,56,21]{1,0,2:T(4,128)S(1)}, f32[4,56,21]{1,0,2:T(4,128)}, u32[]{:S(2)}) %copy-start.9) | copy-done | bytes 18840
  9.7 36.1 %shard_map.136 = f32[9,56,128]{2,1,0:T(8,128)S(1)} custom-call(f32[9,56,128]{2,1,0:T(8,128)S(1)} %copy-done.1, f32[9,9,3,128]{3,2,1,0:T(4,128)S(1)} %bitcast.6, f32[9,9,4,128]{3,2,1,0:T(4,128)S(1)} %bitcast.7, f32[9,9,4,128]{3,2,1,0:T(4,128)S(1)} %bitcast.8, f32[1,128]{1,0:T(1,128)S(1)} %bitcast.11, f32[3,56,56]{2,1,0:T(8,128)S(1)} %copy-done.6, ...), custom_call_target="tpu_custom_call" | custom-call | tf_op jit(solution)/shard_map/pallas_call | solution.py:497
  45.8 0.7 %copy.16 = f32[9,56,128]{2,1,0:T(8,128)} copy(f32[9,56,128]{2,1,0:T(8,128)S(1)} %shard_map.136) | data formatting | bytes 516096
Async XLA Ops:
  0.0 0.7 %copy-start.12 = (s32[4,128]{1,0:T(4,128)S(1)}, s32[4,128]{1,0:T(4,128)}, u32[]{:S(2)}) copy-start(s32[4,128]{1,0:T(4,128)} %orient_ref.1) | copy-start | bytes 6148
  0.0 0.7 %copy-start.10 = (s32[6,64]{1,0:T(8,128)S(1)}, s32[6,64]{1,0:T(8,128)}, u32[]{:S(2)}) copy-start(s32[6,64]{1,0:T(8,128)} %send_ref.1) | copy-start | bytes 4612
  0.0 0.7 %copy-start.11 = (s32[4,128]{1,0:T(4,128)S(1)}, s32[4,128]{1,0:T(4,128)}, u32[]{:S(2)}) copy-start(s32[4,128]{1,0:T(4,128)} %link_ref.1) | copy-start | bytes 6148
  0.0 0.7 %copy-start.13 = (f32[128]{0:T(128)S(1)}, f32[128]{0:T(128)}, u32[]{:S(2)}) copy-start(f32[128]{0:T(128)} %param.18) | copy-start | bytes 1540
  0.7 1.0 %copy-start = (bf16[672,384]{1,0:T(8,128)(2,1)S(1)}, bf16[672,384]{1,0:T(8,128)(2,1)}, u32[]{:S(2)}) copy-start(bf16[672,384]{1,0:T(8,128)(2,1)} %constant.5.clone.rotate_ref) | copy-start | bytes 1548292
  1.8 0.9 %copy-start.1 = (f32[9,56,128]{2,1,0:T(8,128)S(1)}, f32[9,56,128]{2,1,0:T(8,128)}, u32[]{:S(2)}) copy-start(f32[9,56,128]{2,1,0:T(8,128)} %q_ref.1) | copy-start | bytes 774148
  2.7 0.9 %copy-start.2 = (f32[3,9,9,128]{3,0,2,1:T(4,128)S(1)}, f32[3,9,9,128]{3,0,2,1:T(4,128)}, u32[]{:S(2)}) copy-start(f32[3,9,9,128]{3,0,2,1:T(4,128)} %param.15) | copy-start | bytes 373252
  3.6 0.9 %copy-start.3 = (f32[4,9,9,128]{3,0,2,1:T(4,128)S(1)}, f32[4,9,9,128]{3,0,2,1:T(4,128)}, u32[]{:S(2)}) copy-start(f32[4,9,9,128]{3,0,2,1:T(4,128)} %param.16) | copy-start | bytes 497668
  4.5 0.9 %copy-start.4 = (f32[4,9,9,128]{3,0,2,1:T(4,128)S(1)}, f32[4,9,9,128]{3,0,2,1:T(4,128)}, u32[]{:S(2)}) copy-start(f32[4,9,9,128]{3,0,2,1:T(4,128)} %param.17) | copy-start | bytes 497668
  5.5 0.9 %copy-start.5 = (bf16[192,224]{1,0:T(8,128)(2,1)S(1)}, bf16[192,224]{1,0:T(8,128)(2,1)}, u32[]{:S(2)}) copy-start(bf16[192,224]{1,0:T(8,128)(2,1)} %constant.4.clone.compact_ref) | copy-start | bytes 258052
  6.3 0.9 %copy-start.6 = (f32[3,56,56]{2,1,0:T(8,128)S(1)}, f32[3,56,56]{2,1,0:T(8,128)}, u32[]{:S(2)}) copy-start(f32[3,56,56]{2,1,0:T(8,128)} %deriv_ref.1) | copy-start | bytes 112900
  7.2 0.9 %copy-start.7 = (f32[3,56,56]{2,1,0:T(8,128)S(1)}, f32[3,56,56]{2,1,0:T(8,128)}, u32[]{:S(2)}) copy-start(f32[3,56,56]{2,1,0:T(8,128)} %volume_ref.1) | copy-start | bytes 112900
  8.1 0.8 %copy-start.8 = (f32[4,21,56]{2,0,1:T(4,128)S(1)}, f32[4,21,56]{2,0,1:T(4,128)}, u32[]{:S(2)}) copy-start(f32[4,21,56]{2,0,1:T(4,128)} %param.21) | copy-start | bytes 56452
  8.9 0.8 %copy-start.9 = (f32[4,56,21]{1,0,2:T(4,128)S(1)}, f32[4,56,21]{1,0,2:T(4,128)}, u32[]{:S(2)}) copy-start(f32[4,56,21]{1,0,2:T(4,128)} %param.22) | copy-start | bytes 56452
where the time goes:
time: 47 us; the launch traced here: 46.5 us
  Pallas kernels  36.1 us (77%)
  local copies, waits for them, and re-layouts  10.4 us (22%)
    pallas_call x1, Pallas kernels, local(): pl.pallas_call(functools.partial(kernel, count, nq, nb, nf), out_shape=ja...  36.1 us
    unnamed x29, local copies, waits for them, and re-layouts  10.4 us

commit v1 on v0

--- a/solution.py
+++ b/solution.py
@@ -16,6 +16,9 @@
 F32 = jnp.float32
 BF16 = jnp.bfloat16
 MESH = pl.DeviceIdType.MESH
+OPERANDS = 14
+SEND_ORDER = (0, 5, 1, 4, 2, 3)
+GROUP_SPOT = (0, 2, 1)
 
 
 def rotation_table(node_count):
@@ -70,51 +73,60 @@
     nq,
     nb,
     nf,
-    q_ref,
-    star_ref,
-    minus_ref,
-    plus_ref,
-    limit_ref,
-    deriv_ref,
-    volume_ref,
-    proj_ref,
-    lift_ref,
-    link_ref,
-    orient_ref,
-    send_ref,
-    compact_ref,
-    rotate_ref,
-    out_ref,
-    a_der,
-    a_vol,
-    a_proj,
-    a_lift,
-    s_local,
-    s_remote,
-    t_send,
-    series,
-    b_mat,
-    r_mat,
-    vol,
-    own,
-    ic_two,
-    io,
-    faces,
-    pool,
-    picked,
-    turned,
-    across,
-    b_lift,
-    base,
-    min_out,
-    min_in,
-    send_buf,
-    recv_buf,
-    min_send_sem,
-    min_recv_sem,
-    send_sem,
-    recv_sem,
+    *refs,
 ):
+    whole = refs[:OPERANDS]
+    out_ref = refs[OPERANDS]
+    held = refs[OPERANDS + 1 : 2 * OPERANDS + 1]
+    (
+        q_ref,
+        star_ref,
+        minus_ref,
+        plus_ref,
+        limit_ref,
+        deriv_ref,
+        volume_ref,
+        proj_ref,
+        lift_ref,
+        link_ref,
+        orient_ref,
+        send_ref,
+        compact_ref,
+        rotate_ref,
+    ) = held
+    (
+        in_sem,
+        a_der,
+        a_vol,
+        a_proj,
+        a_lift,
+        s_local,
+        s_remote,
+        t_send,
+        series,
+        b_mat,
+        r_mat,
+        vol,
+        own,
+        ic_two,
+        io,
+        faces,
+        pool,
+        picked,
+        turned,
+        across,
+        b_lift,
+        base,
+        star_pair,
+        min_out,
+        min_in,
+        send_buf,
+        recv_buf,
+        min_send_sem,
+        min_recv_sem,
+        send_sem,
+        recv_sem,
+    ) = refs[2 * OPERANDS + 1 :]
     elems = q_ref.shape[2]
     lanes = lax.broadcasted_iota(jnp.int32, (1, elems), 1)
     is_fine = lanes < FINE_DEV
@@ -123,6 +135,12 @@
     rows_c = pool.shape[0] // 2
     half = rows_c // 2
     digits = radices(count)
+
+    def fetch(number):
+        return pltpu.make_async_copy(whole[number], held[number], in_sem.at[number])
+
+    for number in (4, 5, 0, 1, 7, 11, 12, 9, 6, 2, 8, 10, 13, 3):
+        fetch(number).start()
 
     def peer_of(number, step):
         stride = math.prod(digits[:number])
@@ -145,13 +163,6 @@
         def _():
             pl.semaphore_signal(barrier, inc=1, device_id=(target,), device_id_type=MESH)
 
-    least = jnp.where(is_fine, limit_ref[...], limit_ref[...] * 0.5)
-    least = jnp.broadcast_to(jnp.min(least, axis=1, keepdims=True), (8, elems))
-
-    below = jnp.minimum(me, REACH)
-    above = jnp.minimum(count - 1 - me, REACH)
-    pl.semaphore_wait(barrier, expected + below + above)
-
     def min_copy(number, step):
         return pltpu.make_async_remote_copy(
             src_ref=min_out.at[number],
@@ -174,9 +185,6 @@
             value = jnp.minimum(value, min_in[number, step - 1])
         return value
 
-    if digits:
-        min_start(0, least)
-
     def wide(x, width):
         high = x.astype(BF16).astype(F32)
         low = x - high
@@ -187,21 +195,23 @@
             parts = [high, high, low]
         return jnp.concatenate(parts, axis=1)
 
-    for d in range(3):
-        r_mat[d * nb : (d + 1) * nb, 0 : 3 * bp] = wide(deriv_ref[d], bp)
-    a_der[...] = r_mat[0 : 3 * nb, 0 : 3 * bp].astype(BF16)
-    for d in range(3):
-        r_mat[d * nb : (d + 1) * nb, 0 : 3 * bp] = wide(volume_ref[d], bp)
-    a_vol[...] = r_mat[0 : 3 * nb, 0 : 3 * bp].astype(BF16)
-    r_mat[0 : 4 * NODE_PAD, 0 : 3 * bp] = jnp.zeros((4 * NODE_PAD, 3 * bp), F32)
-    for f in range(4):
-        r_mat[f * NODE_PAD : f * NODE_PAD + nf, 0 : 3 * bp] = wide(proj_ref[:, f, :], bp)
-    a_proj[...] = r_mat[0 : 4 * NODE_PAD, 0 : 3 * bp].astype(BF16)
-    r_mat[0 : 4 * NODE_PAD, 0 : 128] = jnp.zeros((4 * NODE_PAD, 128), F32)
-    for f in range(4):
-        r_mat[f * NODE_PAD : f * NODE_PAD + nf, 0:nb] = lift_ref[:, f, :]
-    turned_lift = jnp.transpose(r_mat[0 : 4 * NODE_PAD, 0:128])[0:nb]
-    a_lift[...] = wide(turned_lift, 4 * NODE_PAD).astype(BF16)
+    def square(target, source):
+        for d in range(3):
+            r_mat[d * nb : (d + 1) * nb, 0 : 3 * bp] = wide(source[d], bp)
+        target[...] = r_mat[0 : 3 * nb, 0 : 3 * bp].astype(BF16)
+
+    def make_proj():
+        r_mat[0 : 4 * NODE_PAD, 0 : 3 * bp] = jnp.zeros((4 * NODE_PAD, 3 * bp), F32)
+        for f in range(4):
+            r_mat[f * NODE_PAD : f * NODE_PAD + nf, 0 : 3 * bp] = wide(proj_ref[:, f, :], bp)
+        a_proj[...] = r_mat[0 : 4 * NODE_PAD, 0 : 3 * bp].astype(BF16)
+
+    def make_lift():
+        r_mat[0 : 4 * NODE_PAD, 0:128] = jnp.zeros((4 * NODE_PAD, 128), F32)
+        for f in range(4):
+            r_mat[f * NODE_PAD : f * NODE_PAD + nf, 0:nb] = lift_ref[:, f, :]
+        turned_lift = jnp.transpose(r_mat[0 : 4 * NODE_PAD, 0:128])[0:nb]
+        a_lift[...] = wide(turned_lift, 4 * NODE_PAD).astype(BF16)
 
     def fill(target_q, x):
         high, low = split(jnp.concatenate([x, jnp.zeros((bp - nb, elems), F32)], axis=0))
@@ -209,16 +219,16 @@
         b_mat[bp : 2 * bp, target_q * elems : (target_q + 1) * elems] = low
         b_mat[2 * bp : 3 * bp, target_q * elems : (target_q + 1) * elems] = high
 
-    def starred(a_ref, store):
-        r_mat[...] = dot(a_ref[...], b_mat[...])
+    def starred(a_ref, rows_ref, blocks, store):
+        r_mat[:, 0 : blocks * elems] = dot(a_ref[...], b_mat[:, 0 : blocks * elems])
 
         def group(g, carry):
             sums = [None] * 3
             for d in range(3):
-                for q in range(nq):
+                for q in range(blocks):
                     block = r_mat[d * nb : (d + 1) * nb, q * elems : (q + 1) * elems]
                     for i in range(3):
-                        row = star_ref[g * 3 + i, q, d : d + 1, :]
+                        row = rows_ref[g * 3 + i, q, d : d + 1, :]
                         term = row * block
                         sums[i] = term if sums[i] is None else sums[i] + term
             for i in range(3):
@@ -227,7 +237,7 @@
 
         lax.fori_loop(0, nq // 3, group, 0)
 
-    def taylor():
+    def taylor(first, last):
         def step(k, carry):
             for q in range(nq):
                 fill(q, series[k, q])
@@ -235,53 +245,107 @@
             def keep(p, value):
                 series[k + 1, p] = -value
 
-            starred(a_der, keep)
+            starred(a_der, star_ref, nq, keep)
             return carry
 
+        lax.fori_loop(first, last, step, 0)
+
+    pairs = (nq + 1) // 2
+
+    def taylor_fine():
+        def step(k, carry):
+            for j in range(pairs):
+                fill(j, jnp.where(is_fine, series[k, 2 * j], series[k, min(2 * j + 1, nq - 1)]))
+
+            def keep(p, value):
+                series[k + 1, p] = -(value + pltpu.roll(value, FINE_DEV, 1))
+
+            starred(a_der, star_pair, pairs, keep)
+            return carry
+
         lax.fori_loop(0, ORDER - 1, step, 0)
 
+    numbers = lax.broadcasted_iota(jnp.int32, (128, elems), 0)
+    own_faces = s_local.shape[0]
+
+    def make_sends():
+        for g in range(REACH):
+            sends = jnp.concatenate(
+                [send_ref[2 * g : 2 * g + 1, :], send_ref[2 * g + 1 : 2 * g + 2, :]], axis=1
+            )
+            for v in range(0, own_faces, 128):
+                t_send[v : v + 128, g * elems : (g + 1) * elems] = jnp.where(
+                    numbers + v == sends, 1.0, 0.0
+                ).astype(BF16)
+
+    def make_local():
+        for f in range(4):
+            link = link_ref[f : f + 1, :]
+            for v in range(0, own_faces, 128):
+                s_local[v : v + 128, f * elems : (f + 1) * elems] = jnp.where(
+                    numbers + v == link, 1.0, 0.0
+                ).astype(BF16)
+
+    def make_remote():
+        for f in range(4):
+            link = link_ref[f : f + 1, :]
+            for g in range(REACH):
+                spot = GROUP_SPOT[g] * 128
+                s_remote[spot : spot + 128, f * elems : (f + 1) * elems] = jnp.where(
+                    numbers + (g * 128 + own_faces) == link, 1.0, 0.0
+                ).astype(BF16)
+        for stage in range(2):
+            for position in range(2 * REACH):
+                source = me + offset_of(position)
+
+                @pl.when((source < 0) | (source >= count))
+                def _():
+                    recv_buf[stage, position] = jnp.zeros(recv_buf.shape[2:], F32)
+
+    def make_pairs():
+        def one(p, carry):
+            for j in range(pairs):
+                first = star_ref[p, 2 * j][:, 0:FINE_DEV]
+                if 2 * j + 1 < nq:
+                    second = star_ref[p, 2 * j + 1][:, 0:FINE_DEV]
+                else:
+                    second = jnp.zeros_like(first)
+                star_pair[p, j] = jnp.concatenate([first, second], axis=1)
+            return carry
+
+        lax.fori_loop(0, nq, one, 0)
+
+    fetch(4).wait()
+    least = jnp.where(is_fine, limit_ref[...], limit_ref[...] * 0.5)
+    least = jnp.broadcast_to(jnp.min(least, axis=1, keepdims=True), (8, elems))
+    fetch(5).wait()
+    square(a_der, deriv_ref)
+    fetch(0).wait()
     for q in range(nq):
         series[0, q] = q_ref[q]
-
+    faces[...] = jnp.zeros(faces.shape, F32)
+    below = jnp.minimum(me, REACH)
+    above = jnp.minimum(count - 1 - me, REACH)
+    pl.semaphore_wait(barrier, expected + below + above)
+    if digits:
+        min_start(0, least)
+    fetch(1).wait()
+    taylor(0, 2)
     if digits:
         least = min_finish(0, least)
         if len(digits) > 1:
             min_start(1, least)
-
-    taylor()
-
-    numbers = lax.broadcasted_iota(jnp.int32, (128, elems), 0)
-    own_faces = s_local.shape[0]
-    for f in range(4):
-        link = link_ref[f : f + 1, :]
-        for v in range(0, own_faces, 128):
-            s_local[v : v + 128, f * elems : (f + 1) * elems] = jnp.where(
-                numbers + v == link, 1.0, 0.0
-            ).astype(BF16)
-        for v in range(0, s_remote.shape[0], 128):
-            s_remote[v : v + 128, f * elems : (f + 1) * elems] = jnp.where(
-                numbers + (v + own_faces) == link, 1.0, 0.0
-            ).astype(BF16)
-    for g in range(REACH):
-        sends = jnp.concatenate([send_ref[2 * g : 2 * g + 1, :], send_ref[2 * g + 1 : 2 * g + 2, :]], axis=1)
-        for v in range(0, own_faces, 128):
-            t_send[v : v + 128, g * elems : (g + 1) * elems] = jnp.where(
-                numbers + v == sends, 1.0, 0.0
-            ).astype(BF16)
-    faces[...] = jnp.zeros(faces.shape, F32)
-    for stage in range(2):
-        for position in range(2 * REACH):
-            source = me + offset_of(position)
-
-            @pl.when((source < 0) | (source >= count))
-            def _():
-                recv_buf[stage, position] = jnp.zeros(recv_buf.shape[2:], F32)
-
+    taylor(2, ORDER - 1)
+    fetch(7).wait()
+    make_proj()
+    fetch(11).wait()
+    make_sends()
     for number in range(1, len(digits)):
         least = min_finish(number, least)
         if number + 1 < len(digits):
             min_start(number + 1, least)
     step_fine = least[0:1, :]
+    fetch(12).wait()
 
     weights = []
     weights_two = []
@@ -338,15 +402,19 @@
             upper, lower = packed[0:half], packed[half:rows_c]
             send_buf[stage, 2 * g] = jnp.where(is_fine, upper, pltpu.roll(lower, FINE_DEV, 1))
             send_buf[stage, 2 * g + 1] = jnp.where(is_fine, pltpu.roll(upper, FINE_DEV, 1), lower)
-            for position in (2 * g, 2 * g + 1):
-                target = me - offset_of(position)
-
-                @pl.when((target >= 0) & (target < count))
-                def _():
-                    block_copy(stage, position).start()
-
+        for position in SEND_ORDER:
+            target = me - offset_of(position)
+
+            @pl.when((target >= 0) & (target < count))
+            def _():
+                block_copy(stage, position).start()
+
+        if stage == 0:
+            fetch(9).wait()
+            make_local()
         picked[...] = dot(pool[...], s_local[...])
         if stage == 0:
+            make_remote()
             own[...] = faces[...]
         else:
             for f in range(4):
@@ -357,25 +425,41 @@
         def keep(p, value):
             vol[p] = value
 
-        starred(a_vol, keep)
+        if stage == 0:
+            for number in (6, 2):
+                fetch(number).wait()
+            square(a_vol, volume_ref)
+        starred(a_vol, star_ref, nq, keep)
         flux(minus_ref, own, True)
-
-        for position in range(2 * REACH):
-            source = me + offset_of(position)
-
-            @pl.when((source >= 0) & (source < count))
-            def _():
-                block_copy(stage, position).wait_recv()
-
-        for g in range(REACH):
+        if stage == 0:
+            for number in (8, 10, 13, 3):
+                fetch(number).wait()
+            make_lift()
+            make_pairs()
+
+        def arrive(g):
+            for position in (2 * g, 2 * g + 1):
+                source = me + offset_of(position)
+
+                @pl.when((source >= 0) & (source < count))
+                def _():
+                    block_copy(stage, position).wait_recv()
+
             first, second = recv_buf[stage, 2 * g], recv_buf[stage, 2 * g + 1]
             upper = jnp.where(is_fine, first, pltpu.roll(second, FINE_DEV, 1))
             lower = jnp.where(is_fine, pltpu.roll(first, FINE_DEV, 1), second)
             high, low = split(jnp.concatenate([upper, lower], axis=0))
-            pool[0:rows_c, g * elems : (g + 1) * elems] = high
-            pool[rows_c : 2 * rows_c, g * elems : (g + 1) * elems] = low
+            spot = GROUP_SPOT[g] * elems
+            pool[0:rows_c, spot : spot + elems] = high
+            pool[rows_c : 2 * rows_c, spot : spot + elems] = low
+
         remote = s_remote.shape[0]
-        total = (picked[...] + dot(pool[:, 0:remote], s_remote[...])).astype(BF16)
+        cut = remote - elems
+        arrive(0)
+        arrive(2)
+        picked[...] = picked[...] + dot(pool[:, 0:cut], s_remote[0:cut, :])
+        arrive(1)
+        total = (picked[...] + dot(pool[:, cut:remote], s_remote[cut:remote, :])).astype(BF16)
         rows_n = rotate_ref.shape[0] // 3
         for f in range(4):
             three = dot(rotate_ref[...], total[:, f * elems : (f + 1) * elems])
@@ -408,18 +492,18 @@
         one = weighted(q, weights)
         two = weighted(q, weights_two)
         fill(q, one)
-        ic_two[q] = jnp.where(is_fine, 0.0, two)
-        io[q] = jnp.where(is_fine, 0.0, one + two)
+        ic_two[q] = two
+        io[q] = one + two
     lifted = stage_work(0)
     for p in range(nq):
         mid = q_ref[p] + vol[p] - lifted[:, p * elems : (p + 1) * elems]
         base[p] = jnp.where(is_fine, mid, q_ref[p])
-        series[0, p] = jnp.where(is_fine, mid, 0.0)
-    taylor()
+        series[0, p] = jnp.where(is_fine, mid, pltpu.roll(mid, FINE_DEV, 1))
+    taylor_fine()
     for q in range(nq):
         one = weighted(q, weights)
-        fill(q, one + ic_two[q])
-        io[q] = one + io[q]
+        fill(q, jnp.where(is_fine, one, ic_two[q]))
+        io[q] = jnp.where(is_fine, one, io[q])
     lifted = stage_work(1)
     for p in range(nq):
         out_ref[p] = base[p] + vol[p] - lifted[:, p * elems : (p + 1) * elems]
@@ -463,7 +547,8 @@
     rounds = max(len(radices(count)), 1)
     widest = max([r - 1 for r in radices(count)] + [1])
     vm = pltpu.VMEM
-    scratch = [
+    scratch = [vm(x.shape, x.dtype) for x in args] + [
+        pltpu.SemaphoreType.DMA((OPERANDS,)),
         vm((3 * nb, 3 * bp), BF16),
         vm((3 * nb, 3 * bp), BF16),
         vm((4 * NODE_PAD, 3 * bp), BF16),
@@ -485,6 +570,7 @@
         vm((nq, 4 * NODE_PAD, elems), F32),
         vm((12 * NODE_PAD, nq * elems), BF16),
         vm((nq, nb, elems), F32),
+        vm((nq, (nq + 1) // 2, 3, elems), F32),
         vm((rounds, 8, elems), F32),
         vm((rounds, widest, 8, elems), F32),
         vm((2, 2 * REACH, rows_c // 2, elems), F32),
@@ -497,11 +583,11 @@
     return pl.pallas_call(
         functools.partial(kernel, count, nq, nb, nf),
         out_shape=jax.ShapeDtypeStruct(q_state.shape, F32),
-        in_specs=[pl.BlockSpec(memory_space=pltpu.VMEM)] * len(args),
+        in_specs=[pl.BlockSpec(memory_space=pltpu.HBM)] * len(args),
         out_specs=pl.BlockSpec(memory_space=pltpu.VMEM),
         scratch_shapes=scratch,
         compiler_params=pltpu.CompilerParams(
-            collective_id=0, has_side_effects=True, vmem_limit_bytes=40 * 1024 * 1024
+            collective_id=0, has_side_effects=True, vmem_limit_bytes=62 * 1024 * 1024
         ),
     )(*args)
 

time: 47 us -> 36.6 us (0.78)
  local copies, waits for them, and re-layouts: 10.4 us -> 1.66 us
  Pallas kernels: 36.1 us -> 34.8 us
    unnamed x29 -> x1, local copies, waits for them, and re-layouts: 10.4 us -> 1.66 us
    pallas_call x1, Pallas kernels: 36.1 us -> 34.8 us  [local(): pl.pallas_call(functools.partial(kernel, count, nq, nb, nf), out_shape=ja...]
where the time goes in v1:
time: 36.6 us; the launch traced here: 36.4 us
  Pallas kernels  34.8 us (95%)
  local copies, waits for them, and re-layouts  1.66 us (5%)
    pallas_call x1, Pallas kernels, local(): pl.pallas_call(functools.partial(kernel, count, nq, nb, nf), out_shape=ja...  34.8 us
    unnamed x1, local copies, waits for them, and re-layouts  1.66 us

profile of v1, /device:TPU:0, one launch (start us, length us, event | category | flops | bytes accessed | tf_op | source)
XLA Modules:
  0.0 36.4 jit_solution(17380937660560075753)
XLA Ops:
  0.0 34.8 %shard_map.136 = f32[9,56,128]{2,1,0:T(8,128)} custom-call(f32[9,56,128]{2,1,0:T(8,128)} %refs_0_.1, f32[9,9,3,128]{3,2,1,0:T(4,128)} %bitcast.6, f32[9,9,4,128]{3,2,1,0:T(4,128)} %bitcast.7, f32[9,9,4,128]{3,2,1,0:T(4,128)} %bitcast.8, f32[1,128]{1,0:T(1,128)} %bitcast.11, f32[3,56,56]{2,1,0:T(8,128)} %refs_5_.1, f32[3,56,56]{2,1,0:T(8,128)} %refs_6_.1, ...), custom_call_target="tpu_custom_call" | custom-call | tf_op jit(solution)/shard_map/pallas_call | solution.py:583
  34.8 1.7 %copy.16 = f32[9,56,128]{2,1,0:T(8,128)} copy(f32[9,56,128]{2,1,0:T(8,128)} %shard_map.136) | data formatting | bytes 516096

commit v2 on v1

--- a/solution.py
+++ b/solution.py
@@ -235,7 +235,7 @@
                 store(g * 3 + i, sums[i])
             return carry
 
-        lax.fori_loop(0, nq // 3, group, 0)
+        lax.fori_loop(0, nq // 3, group, 0, unroll=True)
 
     def taylor(first, last):
         def step(k, carry):
@@ -381,7 +381,7 @@
                     across[p, spot, :] = across[p, spot, :] + sums[p]
             return carry
 
-        lax.fori_loop(0, 4, face, 0)
+        lax.fori_loop(0, 4, face, 0, unroll=True)
 
     def stage_work(stage):
         projected = dot(a_proj[...], b_mat[...])

time: 36.6 us -> 35 us (0.956)
  Pallas kernels: 34.8 us -> 33.1 us
    pallas_call x1, Pallas kernels: 34.8 us -> 33.1 us  [local(): pl.pallas_call(functools.partial(kernel, count, nq, nb, nf), out_shape=ja...]
where the time goes in v2:
time: 35 us; the launch traced here: 34.8 us
  Pallas kernels  33.1 us (95%)
  local copies, waits for them, and re-layouts  1.66 us (5%)
    pallas_call x1, Pallas kernels, local(): pl.pallas_call(functools.partial(kernel, count, nq, nb, nf), out_shape=ja...  33.1 us
    unnamed x1, local copies, waits for them, and re-layouts  1.66 us

profile of v2, /device:TPU:0, one launch (start us, length us, event | category | flops | bytes accessed | tf_op | source)
XLA Modules:
  0.0 34.8 jit_solution(7073638209698860280)
XLA Ops:
  0.0 33.1 %shard_map.136 = f32[9,56,128]{2,1,0:T(8,128)} custom-call(f32[9,56,128]{2,1,0:T(8,128)} %refs_0_.1, f32[9,9,3,128]{3,2,1,0:T(4,128)} %bitcast.6, f32[9,9,4,128]{3,2,1,0:T(4,128)} %bitcast.7, f32[9,9,4,128]{3,2,1,0:T(4,128)} %bitcast.8, f32[1,128]{1,0:T(1,128)} %bitcast.11, f32[3,56,56]{2,1,0:T(8,128)} %refs_5_.1, f32[3,56,56]{2,1,0:T(8,128)} %refs_6_.1, ...), custom_call_target="tpu_custom_call" | custom-call | tf_op jit(solution)/shard_map/pallas_call | solution.py:583
  33.1 1.7 %copy.16 = f32[9,56,128]{2,1,0:T(8,128)} copy(f32[9,56,128]{2,1,0:T(8,128)} %shard_map.136) | data formatting | bytes 516096
